TPU v7x, 512 devices: a whole 4x8x8 slice. The times are simulated.
512 devices in a mesh: dp: 16 (over z, core), latent: 32 (over x, y).
Axes of the slice: x: 4, y: 8, z: 8, core: 2. Of those that a mesh axis runs over, the one named last changes fastest.
Arguments:
- activations: bfloat16 [16384, 8192], P('latent', 'dp'), may hold values from -6 to 6
- weight: bfloat16 [8192, 8192], P('dp', 'latent'), may hold values from -0.0625 to 0.0625
- enc_bias: float32 [8192], replicated, may hold values from -3 to 3
- dec_bias: float32 [8192], P('dp'), may hold values from -3 to 3
- block_ids: int32 [32, 8], P('latent'), may hold values from 0 to 63, as said below
- counts: int32 [32], P('latent'), may hold values from 1 to 8, as said below
Outputs:
- weight_grad: float32 [8192, 8192], P('dp', 'latent')
- row_error: float32 [16384], P(('latent', 'dp'))
Inputs may be any that keep to these rules, and one draw needn't show every extreme that they name: `block_ids`: each row block's list names 8 latent blocks of 8 different owners (block k belongs to owner k // 2); only its first counts entries are active, and some blocks are listed far more often than others. `counts`: some row block has all 8 entries active.
All inputs are finite; a program needn't handle non-finite values.
Results may differ from a plain program's by a relative error of at most 0.0028.
Values may be sent and summed in bfloat16 or wider, within the bound.
No kernel may reach another device: no remote copies, remote signals or barrier semaphores. Data moves between devices by JAX's collectives and lax.ppermute only.
A program may use at most 64 MiB of HBM per device.

v0:
```python
import math
import jax
import jax.numpy as jnp
from jax import lax
from jax.sharding import PartitionSpec as P

BLK = 128


def on_device(activations, weight, enc_bias, dec_bias, block_ids, counts):
    rows, width = activations.shape
    block = BLK
    per_owner = weight.shape[1] // block
    owners = lax.axis_size("latent")
    groups = lax.axis_size("dp")
    share = rows // groups
    myself = lax.axis_index("latent")
    all_ids, all_counts = (
        lax.all_gather(block_ids, "latent", axis=0, tiled=True),
        lax.all_gather(counts, "latent", axis=0, tiled=True),
    )
    ids = block_ids[0]
    slots = ids.shape[0]
    live = (jnp.arange(slots) < counts[0]).astype(jnp.float32)
    live_cols = live[:, None, None]
    all_live = (jnp.arange(slots)[None, :] < all_counts[:, None]).astype(jnp.float32)
    own_blocks = myself * per_owner + jnp.arange(per_owner)
    matches = (all_ids[:, :, None] == own_blocks[None, None, :]).astype(jnp.float32) * all_live[
        :, :, None
    ]
    selection = jnp.sum(matches, axis=1).astype(jnp.bfloat16)
    source = (
        (ids[:, None] // per_owner == jnp.arange(owners)[None, :]).astype(jnp.float32)
        * live[:, None]
    ).astype(jnp.bfloat16)
    scale_grad = 2.0 / math.sqrt(rows * owners)
    centered = (activations.astype(jnp.float32) - dec_bias).astype(jnp.bfloat16)
    piece = lax.all_gather(weight, "latent", axis=1, tiled=True)
    number = piece.shape[1] // block
    wanted = (ids[:, None] == jnp.arange(number)[None, :]).astype(jnp.bfloat16)
    picked = jnp.einsum(
        "sb,dbk->sdk",
        wanted,
        piece.reshape(width, number, block),
        preferred_element_type=jnp.float32,
    )
    tiles = picked.astype(jnp.bfloat16)
    bias_rows = jnp.take(enc_bias.reshape(-1, block), ids, axis=0)[:, None, :]
    part_pre = jnp.einsum("rd,sdk->srk", centered, tiles, preferred_element_type=jnp.float32)
    pre = lax.psum(part_pre, "dp") + bias_rows
    act = (jnp.maximum(pre, 0.0) * live_cols).astype(jnp.bfloat16)
    recon = jnp.einsum("srk,sdk->rd", act, tiles, preferred_element_type=jnp.float32) + dec_bias
    err = recon - activations.astype(jnp.float32)
    grad_out = (err * scale_grad).astype(jnp.bfloat16)
    part_loss = jnp.sum(err * err, axis=1) / (width * groups)
    part_grad = jnp.einsum("rd,sdk->srk", grad_out, tiles, preferred_element_type=jnp.float32)
    grad_act, row_total = lax.psum((part_grad, part_loss), "dp")
    grad_pre = (jnp.where(pre > 0, grad_act, 0.0) * live_cols).astype(jnp.bfloat16)
    row_error = lax.dynamic_slice_in_dim(row_total, lax.axis_index("dp") * share, share)
    first = jnp.einsum("rd,srk->sdk", centered, grad_pre, preferred_element_type=jnp.float32)
    second = jnp.einsum("rd,srk->sdk", grad_out, act, preferred_element_type=jnp.float32)
    contribution = (first + second).astype(jnp.bfloat16)
    sending = jnp.einsum(
        "sj,sdk->jdk", source, contribution, preferred_element_type=jnp.float32
    ).astype(jnp.bfloat16)
    received = lax.all_to_all(sending, "latent", split_axis=0, concat_axis=0, tiled=True)
    weight_grad = jnp.einsum("rb,rdk->dbk", selection, received, preferred_element_type=jnp.float32)
    return (weight_grad.reshape(width, per_owner * block), row_error)


def solution(mesh):
    placed = (P("latent", "dp"), P("dp", "latent"), P(), P("dp"), P("latent", None), P("latent"))
    return jax.shard_map(
        on_device,
        mesh=mesh,
        in_specs=placed,
        out_specs=(P("dp", "latent"), P(("latent", "dp"))),
        check_vma=False,
    )
```

profile of v0, /device:TPU:1, one launch (start us, length us, event | category | flops | bytes accessed | tf_op | source)
XLA Modules:
  0.0 583.5 jit_solution(1190068990571921230)
XLA Ops:
  7.2 0.0 copy-start
  7.2 0.0 all-gather.3.cloned.1.call-start
  7.2 0.7 all-gather.3.cloned.1.call-update
  7.9 0.0 all-reduce.4.cloned.1.call-start
  8.0 1.3 copy.19
  9.2 113.8 %all-gather.3.cloned.1.call-done = bf16[512,8192]{1,0:T(8,128)(2,1)} async-done(((bf16[512,256]{1,0:T(8,128)(2,1)}), bf16[512,8192]{1,0:T(8,128)(2,1)}) %all-gather.3.cloned.1.call-update) | async-done | bytes 8388624 | tf_op jit(solution)/shard_map/all_gather | solution.py:38
  123.0 0.0 copy-start.5
  123.0 9.3 %copy.41 = bf16[64,8,64,128]{3,2,1,0:T(8,128)(2,1)} copy(bf16[64,8,64,128]{3,1,2,0:T(8,128)(2,1)} %bitcast.55) | data formatting | bytes 16777216
  132.3 0.0 copy-done.5
  132.3 0.0 copy-start.4
  132.3 4.6 convolution_convert_fusion.1
  136.9 0.0 copy-done.4
  136.9 2.1 convolution_bitcast_fusion.1
  139.1 0.0 all-reduce.4.cloned.1.call-update
  139.1 0.0 all-reduce.6.cloned.1.call-start
  139.8 0.0 copy-done
  139.8 0.6 gather_fusion
  140.4 0.1 broadcast_select_fusion
  140.5 120.1 %all-reduce.4.cloned.1.call-done = f32[8,512,128]{1,2,0:T(8,128)} async-done(((f32[8,512,128]{1,2,0:T(8,128)}), f32[8,512,128]{1,2,0:T(8,128)}) %all-reduce.4.cloned.1.call-update) | async-done | bytes 2097168 | tf_op jit(solution)/shard_map/psum | solution.py:50
  260.6 2.5 multiply_reduce_fusion
  263.1 0.0 copy-start.2
  263.1 1.0 copy-done.2
  264.1 2.1 convolution_bitcast_fusion
  266.1 0.0 copy-start.1
  266.1 0.0 all-reduce.6.cloned.1.call-update
  266.2 120.7 %all-reduce.6.cloned.1.call-done = f32[8,512,128]{1,2,0:T(8,128)} async-done(((f32[8,512,128]{1,2,0:T(8,128)}), f32[8,512,128]{1,2,0:T(8,128)}) %all-reduce.6.cloned.1.call-update) | async-done | bytes 2097168 | tf_op jit(solution)/shard_map/psum | solution.py:57
  386.9 0.0 copy-done.1
  386.9 0.0 copy-start.3
  386.9 2.5 fusion.5
  389.4 0.0 copy-done.3
  389.4 0.8 fusion.2
  390.3 0.8 copy.28
  391.0 1.3 convolution_convert_fusion
  392.4 3.6 copy.29
  396.0 9.4 %all-to-all-start = ((bf16[32,512,128]{2,1,0:T(8,128)(2,1)}), bf16[32,512,128]{2,1,0:T(8,128)(2,1)}, u32[]{:S(2)}, u32[]{:S(2)}) async-start(bf16[32,512,128]{2,1,0:T(8,128)(2,1)} %copy.29), calls=%async_computation | async-start | bytes 8388608 | tf_op jit(solution)/shard_map/all_to_all | solution.py:66
  405.4 116.0 %all-gather = s32[32,1,8]{2,1,0:T(1,128)S(1)} all-gather(s32[1,1,8]{2,1,0:T(1,128)S(1)} %bitcast.60), channel_id=1, replica_groups=mesh['dp'=16,'latent'=32] {'latent'}, dimensions={0}, use_global_device_ids=true | all-gather | bytes 1056 | tf_op jit(solution)/shard_map/all_gather | solution.py:19
  521.4 0.1 copy.30
  521.5 1.3 dynamic-slice
  522.7 0.8 dynamic-update-slice
  523.5 12.8 %all-reduce = s32[32]{0:T(128)S(1)} all-reduce(s32[32]{0:T(128)S(1)} %dynamic-update-slice), channel_id=1, replica_groups=mesh['dp'=16,'latent'=32] {'latent'}, use_global_device_ids=true, to_apply=%add | all-reduce | flops 32 | bytes 256
  536.3 0.1 select_reduce_fusion
  536.4 34.6 %psum.23 = f32[512]{0:T(512)S(1)} all-reduce(f32[512]{0:T(512)S(1)} %broadcast_multiply_fusion), channel_id=1, replica_groups=mesh['dp'=16,'latent'=32] {'dp'}, use_global_device_ids=true, to_apply=%region_4.5 | all-reduce | flops 512 | bytes 4096 | tf_op jit(solution)/shard_map/psum | solution.py:57
  571.0 0.6 dynamic_slice.3
  571.6 0.0 all-to-all-done
  571.6 4.6 fusion
  576.2 0.8 copy.54
  (9 shorter events, 0.0 us)
Async XLA Ops:
  7.2 132.6 %copy-start = (f32[8192]{0:T(1024)S(1)}, f32[8192]{0:T(1024)}, u32[]{:S(2)}) copy-start(f32[8192]{0:T(1024)} %param.8) | copy-start | bytes 98308
  7.2 115.8 %all-gather.3.cloned.1.call-start = ((), (), s32[]{:S(2)}) async-start(), calls=%async_computation.1 | async-start | bytes 8650752 | tf_op jit(solution)/shard_map/all_gather | solution.py:38
  7.9 252.7 %all-reduce.4.cloned.1.call-start = ((), (), s32[]{:S(2)}) async-start(), calls=%async_computation.2 | async-start | bytes 4194304 | tf_op jit(solution)/shard_map/psum | solution.py:50
  123.0 9.3 %copy-start.5 = (s32[1,8]{1,0:T(1,128)S(1)}, s32[1,8]{1,0:T(1,128)}, u32[]{:S(2)}) copy-start(s32[1,8]{1,0:T(1,128)} %param.10) | copy-start | bytes 100
  132.3 4.6 copy-start.4
  139.1 247.8 %all-reduce.6.cloned.1.call-start = ((), (), s32[]{:S(2)}) async-start(), calls=%async_computation.3 | async-start | bytes 4194304 | tf_op jit(solution)/shard_map/psum | solution.py:57
  263.1 1.0 copy-start.2
  266.1 120.8 %copy-start.1 = (f32[8,512,128]{1,2,0:T(8,128)S(1)}, f32[8,512,128]{1,2,0:T(8,128)}, u32[]{:S(2)}) copy-start(f32[8,512,128]{1,2,0:T(8,128)} %all-reduce.4.cloned.1.call-done) | copy-start | bytes 6291460
  386.9 2.6 copy-start.3
  396.0 175.6 %all-to-all-start = ((bf16[32,512,128]{2,1,0:T(8,128)(2,1)}), bf16[32,512,128]{2,1,0:T(8,128)(2,1)}, u32[]{:S(2)}, u32[]{:S(2)}) async-start(bf16[32,512,128]{2,1,0:T(8,128)(2,1)} %copy.29), calls=%async_computation | async-start | bytes 8388608 | tf_op jit(solution)/shard_map/all_to_all | solution.py:66
Sparse Core Ops, SparseCore 0:
  11.1 111.8 all-gather.2
  139.2 121.3 all-reduce.3
  266.3 120.5 all-reduce.5
where the time goes:
time: 584 us
  waiting for transfers between devices  355 us (61%)
  blocking collectives  163 us (28%)
  matrix products  20.6 us (4%)
  local copies, waits for them, and re-layouts  20 us (3%)
  between operations  14.5 us (2%)
  starting transfers between devices  9.52 us (2%)
    psum x1, waiting for transfers between devices, on_device(): grad_act, row_total = lax.psum((part_grad, part_loss), 'dp')  121 us
    psum x1, waiting for transfers between devices, on_device(): pre = lax.psum(part_pre, 'dp') + bias_rows  120 us
    all_gather x1, blocking collectives, on_device(): lax.all_gather(block_ids, 'latent', axis=0, tiled=True)  116 us
    all_gather x1, waiting for transfers between devices, on_device(): piece = lax.all_gather(weight, 'latent', axis=1, tiled=True)  114 us
    psum x1, blocking collectives, on_device(): grad_act, row_total = lax.psum((part_grad, part_loss), 'dp')  34.6 us
    unnamed x19, local copies, waits for them, and re-layouts  14.5 us
    unnamed x1, blocking collectives  12.8 us
  transfers between devices with their start and end apart: 4, of which 3 were waited for; matrix products, arithmetic and copies ran while one was open for 1% of the time, Pallas kernels for 0%

commit v1 on v0

--- a/solution.py
+++ b/solution.py
@@ -16,7 +16,9 @@
     share = rows // groups
     myself = lax.axis_index("latent")
     all_ids, all_counts = (
-        lax.all_gather(block_ids, "latent", axis=0, tiled=True),
+        jnp.concatenate(
+            lax.all_to_all(jnp.stack([block_ids] * lax.axis_size("latent")), "latent", 0, 0), axis=0
+        ),
         lax.all_gather(counts, "latent", axis=0, tiled=True),
     )
     ids = block_ids[0]

time: 584 us -> 551 us (0.943)
  blocking collectives: 163 us -> 130 us
  waiting for transfers between devices: 355 us -> 345 us
  starting transfers between devices: 9.52 us -> 18.8 us
    all_gather x1 -> x0, blocking collectives: 116 us -> none  [on_device(): lax.all_gather(block_ids, 'latent', axis=0, tiled=True)]
    unnamed x1, blocking collectives: 12.8 us -> 103 us
    psum x1, waiting for transfers between devices: 121 us -> 111 us  [on_device(): grad_act, row_total = lax.psum((part_grad, part_loss), 'dp')]
    all_to_all x0 -> x1, starting transfers between devices: none -> 9.26 us  [on_device(): lax.all_to_all(jnp.stack([block_ids] * lax.axis_size('latent')), 'latent'...]
    psum x1, blocking collectives: 34.6 us -> 27 us  [on_device(): grad_act, row_total = lax.psum((part_grad, part_loss), 'dp')]
    unnamed x19 -> x18, local copies, waits for them, and re-layouts: 14.5 us -> 14.4 us
  transfers between devices with their start and end apart: 4 -> 5, of which waited for: 3 -> 3; matrix products, arithmetic and copies ran while one was open for 1% -> 3% of each run, Pallas kernels for 0% -> 0%
where the time goes in v1:
time: 551 us; the launch traced here: 550 us
  waiting for transfers between devices  345 us (63%)
  blocking collectives  130 us (24%)
  local copies, waits for them, and re-layouts  20.6 us (4%)
  matrix products  20.6 us (4%)
  starting transfers between devices  18.8 us (3%)
  between operations  14.5 us (3%)
    psum x1, waiting for transfers between devices, on_device(): pre = lax.psum(part_pre, 'dp') + bias_rows  120 us
    all_gather x1, waiting for transfers between devices, on_device(): piece = lax.all_gather(weight, 'latent', axis=1, tiled=True)  114 us
    psum x1, waiting for transfers between devices, on_device(): grad_act, row_total = lax.psum((part_grad, part_loss), 'dp')  111 us
    unnamed x1, blocking collectives  103 us
    psum x1, blocking collectives, on_device(): grad_act, row_total = lax.psum((part_grad, part_loss), 'dp')  27 us
    unnamed x18, local copies, waits for them, and re-layouts  14.4 us
  transfers between devices with their start and end apart: 5, of which 3 were waited for; matrix products, arithmetic and copies ran while one was open for 3% of the time, Pallas kernels for 0%

profile of v1, /device:TPU:1, one launch (start us, length us, event | category | flops | bytes accessed | tf_op | source)
XLA Modules:
  0.0 550.1 jit_solution(3317843526871270815)
XLA Ops:
  7.2 0.0 copy-start
  7.2 0.0 all-gather.2.cloned.1.call-start
  7.2 0.7 all-gather.2.cloned.1.call-update
  7.9 0.0 all-reduce.4.cloned.1.call-start
  8.0 1.3 copy.31
  9.2 113.8 %all-gather.2.cloned.1.call-done = bf16[512,8192]{1,0:T(8,128)(2,1)} async-done(((bf16[512,256]{1,0:T(8,128)(2,1)}), bf16[512,8192]{1,0:T(8,128)(2,1)}) %all-gather.2.cloned.1.call-update) | async-done | bytes 8388624 | tf_op jit(solution)/shard_map/all_gather | solution.py:40
  123.0 0.0 copy-start.5
  123.0 9.3 %copy.53 = bf16[64,8,64,128]{3,2,1,0:T(8,128)(2,1)} copy(bf16[64,8,64,128]{3,1,2,0:T(8,128)(2,1)} %bitcast.54) | data formatting | bytes 16777216
  132.3 0.0 copy-done.5
  132.3 0.0 copy-start.4
  132.3 4.6 convolution_convert_fusion.1
  136.9 0.0 copy-done.4
  137.0 2.1 convolution_bitcast_fusion.1
  139.1 0.0 all-reduce.4.cloned.1.call-update
  139.1 0.0 all-reduce.6.cloned.1.call-start
  139.8 0.0 copy-done
  139.8 0.6 gather_fusion
  140.4 0.1 broadcast_select_fusion
  140.5 120.1 %all-reduce.4.cloned.1.call-done = f32[8,512,128]{1,2,0:T(8,128)} async-done(((f32[8,512,128]{1,2,0:T(8,128)}), f32[8,512,128]{1,2,0:T(8,128)}) %all-reduce.4.cloned.1.call-update) | async-done | bytes 2097168 | tf_op jit(solution)/shard_map/psum | solution.py:52
  260.6 2.5 multiply_reduce_fusion
  263.1 0.0 copy-start.2
  263.1 1.0 copy-done.2
  264.1 2.1 convolution_bitcast_fusion
  266.1 0.0 copy-start.1
  266.1 0.0 all-reduce.6.cloned.1.call-update
  266.2 0.6 stack.2
  266.8 9.3 %all-to-all-start.1 = ((s32[32,1,8]{2,1,0:T(1,128)}), s32[32,1,8]{2,1,0:T(1,128)S(1)}, u32[]{:S(2)}, u32[]{:S(2)}) async-start(s32[32,1,8]{2,1,0:T(1,128)} %stack.2), calls=%async_computation.1 | async-start | bytes 32768 | tf_op jit(solution)/shard_map/all_to_all | solution.py:20
  276.1 110.8 %all-reduce.6.cloned.1.call-done = f32[8,512,128]{1,2,0:T(8,128)} async-done(((f32[8,512,128]{1,2,0:T(8,128)}), f32[8,512,128]{1,2,0:T(8,128)}) %all-reduce.6.cloned.1.call-update) | async-done | bytes 2097168 | tf_op jit(solution)/shard_map/psum | solution.py:59
  386.9 0.0 copy-done.1
  386.9 0.0 copy-start.3
  386.9 2.5 fusion.5
  389.4 0.0 copy-done.3
  389.4 0.8 fusion.2
  390.3 0.8 copy.40
  391.0 1.3 convolution_convert_fusion
  392.4 3.6 copy.41
  396.0 0.0 all-to-all-done.1
  396.0 9.4 %all-to-all-start = ((bf16[32,512,128]{2,1,0:T(8,128)(2,1)}), bf16[32,512,128]{2,1,0:T(8,128)(2,1)}, u32[]{:S(2)}, u32[]{:S(2)}) async-start(bf16[32,512,128]{2,1,0:T(8,128)(2,1)} %copy.41), calls=%async_computation | async-start | bytes 8388608 | tf_op jit(solution)/shard_map/all_to_all | solution.py:68
  405.4 1.3 dynamic-slice
  406.7 0.8 dynamic-update-slice
  407.4 103.0 %all-reduce = s32[32]{0:T(128)S(1)} all-reduce(s32[32]{0:T(128)S(1)} %dynamic-update-slice), channel_id=1, replica_groups=mesh['dp'=16,'latent'=32] {'latent'}, use_global_device_ids=true, to_apply=%add | all-reduce | flops 32 | bytes 256
  510.4 0.1 copy.42
  510.5 0.1 select_reduce_fusion
  510.6 27.0 %psum.23 = f32[512]{0:T(512)S(1)} all-reduce(f32[512]{0:T(512)S(1)} %broadcast_multiply_fusion), channel_id=1, replica_groups=mesh['dp'=16,'latent'=32] {'dp'}, use_global_device_ids=true, to_apply=%region_4.5 | all-reduce | flops 512 | bytes 4096 | tf_op jit(solution)/shard_map/psum | solution.py:59
  537.6 0.6 dynamic_slice.3
  538.2 0.0 all-to-all-done
  538.2 4.6 fusion
  542.8 0.8 copy.66
  (9 shorter events, 0.0 us)
Async XLA Ops:
  7.2 132.7 %copy-start = (f32[8192]{0:T(1024)S(1)}, f32[8192]{0:T(1024)}, u32[]{:S(2)}) copy-start(f32[8192]{0:T(1024)} %param.8) | copy-start | bytes 98308
  7.2 115.8 %all-gather.2.cloned.1.call-start = ((), (), s32[]{:S(2)}) async-start(), calls=%async_computation.2 | async-start | bytes 8650752 | tf_op jit(solution)/shard_map/all_gather | solution.py:40
  7.9 252.7 %all-reduce.4.cloned.1.call-start = ((), (), s32[]{:S(2)}) async-start(), calls=%async_computation.3 | async-start | bytes 4194304 | tf_op jit(solution)/shard_map/psum | solution.py:52
  123.0 9.3 %copy-start.5 = (s32[1,8]{1,0:T(1,128)S(1)}, s32[1,8]{1,0:T(1,128)}, u32[]{:S(2)}) copy-start(s32[1,8]{1,0:T(1,128)} %param.10) | copy-start | bytes 100
  132.3 4.6 copy-start.4
  139.1 247.8 %all-reduce.6.cloned.1.call-start = ((), (), s32[]{:S(2)}) async-start(), calls=%async_computation.4 | async-start | bytes 4194304 | tf_op jit(solution)/shard_map/psum | solution.py:59
  263.1 1.0 copy-start.2
  266.1 120.8 %copy-start.1 = (f32[8,512,128]{1,2,0:T(8,128)S(1)}, f32[8,512,128]{1,2,0:T(8,128)}, u32[]{:S(2)}) copy-start(f32[8,512,128]{1,2,0:T(8,128)} %all-reduce.4.cloned.1.call-done) | copy-start | bytes 6291460
  266.8 129.2 %all-to-all-start.1 = ((s32[32,1,8]{2,1,0:T(1,128)}), s32[32,1,8]{2,1,0:T(1,128)S(1)}, u32[]{:S(2)}, u32[]{:S(2)}) async-start(s32[32,1,8]{2,1,0:T(1,128)} %stack.2), calls=%async_computation.1 | async-start | bytes 32768 | tf_op jit(solution)/shard_map/all_to_all | solution.py:20
  386.9 2.6 copy-start.3
  396.0 142.2 %all-to-all-start = ((bf16[32,512,128]{2,1,0:T(8,128)(2,1)}), bf16[32,512,128]{2,1,0:T(8,128)(2,1)}, u32[]{:S(2)}, u32[]{:S(2)}) async-start(bf16[32,512,128]{2,1,0:T(8,128)(2,1)} %copy.41), calls=%async_computation | async-start | bytes 8388608 | tf_op jit(solution)/shard_map/all_to_all | solution.py:68
Sparse Core Ops, SparseCore 0:
  11.1 111.8 all-gather.1
  139.2 121.3 all-reduce.3
  266.3 120.5 all-reduce.5

commit v2 on v0

--- a/solution.py
+++ b/solution.py
@@ -47,7 +47,7 @@
     tiles = picked.astype(jnp.bfloat16)
     bias_rows = jnp.take(enc_bias.reshape(-1, block), ids, axis=0)[:, None, :]
     part_pre = jnp.einsum("rd,sdk->srk", centered, tiles, preferred_element_type=jnp.float32)
-    pre = lax.psum(part_pre, "dp") + bias_rows
+    pre = jnp.sum(lax.all_gather(part_pre, "dp"), axis=0) + bias_rows
     act = (jnp.maximum(pre, 0.0) * live_cols).astype(jnp.bfloat16)
     recon = jnp.einsum("srk,sdk->rd", act, tiles, preferred_element_type=jnp.float32) + dec_bias
     err = recon - activations.astype(jnp.float32)

time: 584 us -> 654 us (1.12)
  waiting for transfers between devices: 355 us -> 410 us
  other arithmetic: 0.2 us -> 13.2 us
    all_gather x0 -> x1, waiting for transfers between devices: none -> 178 us  [on_device(): pre = jnp.sum(lax.all_gather(part_pre, 'dp'), axis=0) + bias_rows]
    psum x1 -> x0, waiting for transfers between devices: 120 us -> none  [on_device(): pre = lax.psum(part_pre, 'dp') + bias_rows]
    reduce_sum x0 -> x1, other arithmetic: none -> 13 us  [on_device(): pre = jnp.sum(lax.all_gather(part_pre, 'dp'), axis=0) + bias_rows]
    unnamed x19 -> x24, local copies, waits for them, and re-layouts: 14.5 us -> 17.2 us
where the time goes in v2:
time: 654 us
  waiting for transfers between devices  410 us (63%)
  blocking collectives  163 us (25%)
  local copies, waits for them, and re-layouts  24.5 us (4%)
  matrix products  18.8 us (3%)
  between operations  14.5 us (2%)
  other arithmetic  13.2 us (2%)
  starting transfers between devices  9.51 us (1%)
    all_gather x1, waiting for transfers between devices, on_device(): pre = jnp.sum(lax.all_gather(part_pre, 'dp'), axis=0) + bias_rows  178 us
    psum x1, waiting for transfers between devices, on_device(): grad_act, row_total = lax.psum((part_grad, part_loss), 'dp')  119 us
    all_gather x1, blocking collectives, on_device(): lax.all_gather(block_ids, 'latent', axis=0, tiled=True)  116 us
    all_gather x1, waiting for transfers between devices, on_device(): piece = lax.all_gather(weight, 'latent', axis=1, tiled=True)  113 us
    psum x1, blocking collectives, on_device(): grad_act, row_total = lax.psum((part_grad, part_loss), 'dp')  34.4 us
    unnamed x24, local copies, waits for them, and re-layouts  17.2 us
  transfers between devices with their start and end apart: 4, of which 3 were waited for; matrix products, arithmetic and copies ran while one was open for 1% of the time, Pallas kernels for 0%

profile of v2, /device:TPU:1, one launch (start us, length us, event | category | flops | bytes accessed | tf_op | source)
XLA Modules:
  0.0 653.7 jit_solution(8552971366417559309)
XLA Ops:
  7.2 0.0 copy-start
  7.2 0.0 all-gather.5.cloned.1.call-start
  7.2 0.7 all-gather.5.cloned.1.call-update
  7.9 0.0 all-gather.7.cloned.1.call-start
  8.0 2.0 copy.20
  10.0 113.0 %all-gather.5.cloned.1.call-done = bf16[512,8192]{1,0:T(8,128)(2,1)} async-done(((bf16[512,256]{1,0:T(8,128)(2,1)}), bf16[512,8192]{1,0:T(8,128)(2,1)}) %all-gather.5.cloned.1.call-update) | async-done | bytes 8388624 | tf_op jit(solution)/shard_map/all_gather | solution.py:38
  123.0 0.0 copy-start.7
  123.0 9.3 %copy.45 = bf16[64,8,64,128]{3,2,1,0:T(8,128)(2,1)} copy(bf16[64,8,64,128]{3,1,2,0:T(8,128)(2,1)} %bitcast.57) | data formatting | bytes 16777216
  132.3 0.0 copy-done.7
  132.3 0.0 copy-start.2
  132.3 4.7 convolution_convert_fusion.1
  137.0 0.0 copy-done.2
  137.0 0.0 copy-done.6
  137.0 0.8 convolution_bitcast_fusion.1
  137.8 1.8 copy.23
  139.7 0.0 all-gather.7.cloned.1.call-update
  139.7 0.0 all-reduce.3.cloned.1.call-start
  140.4 0.0 copy-done
  140.4 0.6 gather_fusion
  141.0 0.1 broadcast_select_fusion
  141.1 177.6 %all-gather.7.cloned.1.call-done = f32[128,512,128]{2,1,0:T(8,128)} async-done(((f32[8,512,128]{2,1,0:T(8,128)}), f32[128,512,128]{2,1,0:T(8,128)}) %all-gather.7.cloned.1.call-update) | async-done | bytes 33554448 | tf_op jit(solution)/shard_map/all_gather | solution.py:50
  318.7 13.0 %reduce_sum.27 = f32[8,512,128]{2,1,0:T(8,128)} reduce(f32[16,8,512,128]{3,2,1,0:T(8,128)} %bitcast.55, f32[]{:T(128)} %constant.42.clone.1), dimensions={0}, to_apply=%region_0.0 | reduce | flops 7864320 | bytes 35651588 | tf_op jit(solution)/shard_map/reduce_sum | solution.py:50
  331.7 1.9 copy.44
  333.6 1.9 multiply_reduce_fusion
  335.6 1.0 copy-done.4
  336.5 2.1 convolution_bitcast_fusion
  338.6 0.0 all-reduce.3.cloned.1.call-update
  338.6 118.6 %all-reduce.3.cloned.1.call-done = f32[8,512,128]{1,2,0:T(8,128)} async-done(((f32[8,512,128]{1,2,0:T(8,128)}), f32[8,512,128]{1,2,0:T(8,128)}) %all-reduce.3.cloned.1.call-update) | async-done | bytes 2097168 | tf_op jit(solution)/shard_map/psum | solution.py:57
  457.3 0.0 copy-done.3
  457.3 2.5 fusion.5
  459.8 0.0 copy-done.5
  459.8 0.8 fusion.2
  460.6 0.8 copy.31
  461.4 1.3 convolution_convert_fusion
  462.8 3.6 copy.32
  466.3 9.4 %all-to-all-start = ((bf16[32,512,128]{2,1,0:T(8,128)(2,1)}), bf16[32,512,128]{2,1,0:T(8,128)(2,1)}, u32[]{:S(2)}, u32[]{:S(2)}) async-start(bf16[32,512,128]{2,1,0:T(8,128)(2,1)} %copy.32), calls=%async_computation | async-start | bytes 8388608 | tf_op jit(solution)/shard_map/all_to_all | solution.py:66
  475.8 116.0 %all-gather.1 = s32[32,1,8]{2,1,0:T(1,128)S(1)} all-gather(s32[1,1,8]{2,1,0:T(1,128)S(1)} %bitcast.62), channel_id=1, replica_groups=mesh['dp'=16,'latent'=32] {'latent'}, dimensions={0}, use_global_device_ids=true | all-gather | bytes 1056 | tf_op jit(solution)/shard_map/all_gather | solution.py:19
  591.8 0.1 copy.33
  591.8 1.3 dynamic-slice
  593.1 0.8 dynamic-update-slice
  593.9 12.8 %all-reduce = s32[32]{0:T(128)S(1)} all-reduce(s32[32]{0:T(128)S(1)} %dynamic-update-slice), channel_id=1, replica_groups=mesh['dp'=16,'latent'=32] {'latent'}, use_global_device_ids=true, to_apply=%add | all-reduce | flops 32 | bytes 256
  606.6 0.1 select_reduce_fusion
  606.7 34.4 %psum.15 = f32[512]{0:T(512)S(1)} all-reduce(f32[512]{0:T(512)S(1)} %broadcast_multiply_fusion), channel_id=1, replica_groups=mesh['dp'=16,'latent'=32] {'dp'}, use_global_device_ids=true, to_apply=%region_4.5 | all-reduce | flops 512 | bytes 4096 | tf_op jit(solution)/shard_map/psum | solution.py:57
  641.2 0.6 dynamic_slice.3
  641.8 0.0 all-to-all-done
  641.8 4.6 fusion
  646.4 0.8 copy.58
  647.2 0.0 copy-done.1
  (14 shorter events, 0.1 us)
Async XLA Ops:
  7.2 133.2 %copy-start = (f32[8192]{0:T(1024)S(1)}, f32[8192]{0:T(1024)}, u32[]{:S(2)}) copy-start(f32[8192]{0:T(1024)} %param.8) | copy-start | bytes 98308
  7.2 115.8 %all-gather.5.cloned.1.call-start = ((), (), s32[]{:S(2)}) async-start(), calls=%async_computation.1 | async-start | bytes 8650752 | tf_op jit(solution)/shard_map/all_gather | solution.py:38
  7.9 310.7 %all-gather.7.cloned.1.call-start = ((), (), s32[]{:S(2)}) async-start(), calls=%async_computation.3 | async-start | bytes 35651584 | tf_op jit(solution)/shard_map/all_gather | solution.py:50
  123.0 9.3 %copy-start.7 = (s32[1,8]{1,0:T(1,128)S(1)}, s32[1,8]{1,0:T(1,128)}, u32[]{:S(2)}) copy-start(s32[1,8]{1,0:T(1,128)} %param.10) | copy-start | bytes 100
  132.3 4.7 copy-start.2
  132.3 4.7 copy-start.6
  139.7 317.6 %all-reduce.3.cloned.1.call-start = ((), (), s32[]{:S(2)}) async-start(), calls=%async_computation.2 | async-start | bytes 4194304 | tf_op jit(solution)/shard_map/psum | solution.py:57
  335.6 1.0 copy-start.4
  338.6 118.7 %copy-start.3 = (bf16[512,512]{0,1:T(8,128)(2,1)S(1)}, bf16[512,512]{0,1:T(8,128)(2,1)}, u32[]{:S(2)}) copy-start(bf16[512,512]{0,1:T(8,128)(2,1)} %copy.20) | copy-start | bytes 1572868
  457.3 2.6 copy-start.5
  466.3 175.4 %all-to-all-start = ((bf16[32,512,128]{2,1,0:T(8,128)(2,1)}), bf16[32,512,128]{2,1,0:T(8,128)(2,1)}, u32[]{:S(2)}, u32[]{:S(2)}) async-start(bf16[32,512,128]{2,1,0:T(8,128)(2,1)} %copy.32), calls=%async_computation | async-start | bytes 8388608 | tf_op jit(solution)/shard_map/all_to_all | solution.py:66
  641.2 6.0 copy-start.1
Sparse Core Ops, SparseCore 0:
  11.1 111.8 all-gather.4
  139.8 178.8 all-gather.6
  338.8 118.4 all-reduce.2
